TPU v7x, 32 devices: a whole 2x2x4 slice. The times are simulated.
32 devices in a mesh: vox: 8 (over y, x, core), load: 4 (over z).
Axes of the slice: x: 2, y: 2, z: 4, core: 2. Of those that a mesh axis runs over, the one named last changes fastest.
Arguments:
- reduced_shape_matrix: bfloat16 [8192, 512], P('vox'), may hold values from -0.25 to 0.25
- young_modulus: float32 [8192], P('vox'), may hold values from 0.5 to 2
- work_stiffening_modulus: float32 [8192], P('vox'), may hold values from 0.2 to 2
- entry_flow_stress: float32 [8192], P('vox'), may hold values from 0.5 to 2
- dilation_factor: float32 [8192], P('vox'), may hold values from 0.5 to 2
- heat_difference: float32 [512], P('load'), may hold values from -4 to 4
- flowing_entry_flags: int32 [8192, 512], P('vox', 'load'), may hold values 0 or 1
- starting_permanent_deformation: float32 [8192, 512], P('vox', 'load'), may hold values from -3 to 3
- starting_weights: float32 [512, 512], P('vox', 'load'), may hold values from -5 to 5
- applied_reduced_vector: float32 [512, 512], P('vox', 'load'), may hold values from -96 to 96
- approx_tangent_inverse: float32 [512, 512], replicated, as said below
Outputs:
- final_mode_coefficients: float32 [512, 512], P('vox', 'load')
- strain_out: float32 [8192, 512], P('vox', 'load')
Inputs may be any that keep to these rules, and one draw needn't show every extreme that they name: `approx_tangent_inverse`: it has a positive diagonal.
All inputs are finite; a program needn't handle non-finite values. No bound on the sum of `flowing_entry_flags` on one device may be relied on, other than what follows from the above.
Results may differ from a plain program's by a relative error of at most 0.0013.
Values may be sent and summed in bfloat16 or wider, within the bound.
A program may use at most 64 MiB of HBM per device.

v0:
```python
import jax
import jax.numpy as jnp
from jax import lax
from jax.sharding import PartitionSpec as P

M = 512
ITERS = 3


def shards(
    reduced_shape_matrix,
    young_modulus,
    work_stiffening_modulus,
    entry_flow_stress,
    dilation_factor,
    heat_difference,
    flowing_entry_flags,
    starting_permanent_deformation,
    starting_weights,
    applied_reduced_vector,
    approx_tangent_inverse,
):
    own_rows = starting_weights.shape[0]
    points = starting_weights.shape[1]
    load_point_total = points * lax.axis_size("load")
    plastic = starting_permanent_deformation
    active = flowing_entry_flags.astype(jnp.float32)
    modulus = young_modulus[:, None]
    harden = work_stiffening_modulus[:, None]
    yielded = entry_flow_stress[:, None]
    heating_history = dilation_factor[:, None] * heat_difference[None, :]
    xi_now, force_all = (
        lax.all_gather(starting_weights, "vox", axis=0, tiled=True),
        lax.all_gather(applied_reduced_vector, "vox", axis=0, tiled=True),
    )
    for sweep in range(ITERS):
        strain = jnp.dot(
            reduced_shape_matrix, xi_now.astype(jnp.bfloat16), preferred_element_type=jnp.float32
        )
        trial = modulus * (strain - heating_history - plastic)
        excess = trial - yielded * jnp.tanh(trial / yielded)
        increment = active * excess / (modulus + harden)
        stress = (trial - modulus * increment).astype(jnp.bfloat16)
        stress, plastic = (stress, plastic + increment)
        partial_sum = lax.dot_general(
            reduced_shape_matrix,
            stress,
            (((0,), (0,)), ((), ())),
            preferred_element_type=jnp.float32,
        )
        resid = lax.psum(partial_sum, "vox") - force_all
        delta = jnp.dot(approx_tangent_inverse, resid, precision=lax.Precision.HIGHEST)
        spread = lax.psum(jnp.sum(delta * delta), "load") / (M * load_point_total)
        xi_now = xi_now - delta / (1.0 + spread)
    mine = lax.dynamic_slice_in_dim(xi_now, lax.axis_index("vox") * own_rows, own_rows, 0)
    return (mine, plastic)


def solution(mesh):
    in_specs = (
        P("vox", None),
        P("vox"),
        P("vox"),
        P("vox"),
        P("vox"),
        P("load"),
        P("vox", "load"),
        P("vox", "load"),
        P("vox", "load"),
        P("vox", "load"),
        P(),
    )
    out_specs = (P("vox", "load"), P("vox", "load"))
    return jax.shard_map(shards, mesh=mesh, in_specs=in_specs, out_specs=out_specs, check_vma=False)
```

profile of v0, /device:TPU:0, one launch (start us, length us, event | category | flops | bytes accessed | tf_op | source)
XLA Modules:
  0.0 242.3 jit_solution(9750270543719354730)
XLA Ops:
  7.2 11.1 %all_gather.6 = f32[512,128]{1,0:T(8,128)S(1)} all-gather(f32[64,128]{1,0:T(8,128)} %param.19), channel_id=1, replica_groups=mesh['vox'=8,'load'=4] {'vox'}, dimensions={0}, use_global_device_ids=true | all-gather | bytes 294912 | tf_op jit(solution)/shard_map/all_gather | solution.py:33
  18.4 0.7 copy-done.8
  19.1 1.5 fusion.1
  20.6 0.8 copy-done.4
  21.4 1.7 convolution_bitcast_fusion.4
  23.2 0.1 copy.17
  23.3 9.4 %all_gather.7 = f32[512,128]{1,0:T(8,128)S(1)} all-gather(f32[64,128]{1,0:T(8,128)S(1)} %copy-done.6), channel_id=1, replica_groups=mesh['vox'=8,'load'=4] {'vox'}, dimensions={0}, use_global_device_ids=true | all-gather | bytes 294912 | tf_op jit(solution)/shard_map/all_gather | solution.py:34
  32.7 44.4 %all-reduce.4.cloned.1.call-done = f32[512,128]{1,0:T(8,128)} async-done(((f32[512,128]{1,0:T(8,128)}), f32[512,128]{1,0:T(8,128)}) %all-reduce.4.cloned.1.call-update) | async-done | bytes 262160 | tf_op jit(solution)/shard_map/psum | solution.py:51
  77.2 2.6 %multiply_reduce_fusion.2 = (f32[]{:T(128)}, f32[128,512]{1,0:T(8,128)S(1)}) fusion(f32[512,512]{1,0:T(8,128)S(1)} %copy-done.1, f32[512,128]{1,0:T(8,128)} %all-reduce.4.cloned.1.call-done, f32[512,128]{1,0:T(8,128)S(1)} %all_gather.7), kind=kOutput, calls=%fused_computation.29 | convolution fusion | flops 402849792 | bytes 1835012 | tf_op jit(solution)/shard_map/dot_general | solution.py:52
  79.8 12.3 %psum.43 = f32[]{:T(128)} all-reduce(f32[]{:T(128)} %get-tuple-element.6), channel_id=1, replica_groups=mesh['vox'=8,'load'=4] {'load'}, use_global_device_ids=true, to_apply=%region_2.0 | all-reduce | flops 1 | bytes 8 | tf_op jit(solution)/shard_map/psum | solution.py:53
  92.7 2.1 fusion.7
  94.8 0.8 copy-done.15
  95.6 1.7 convolution_bitcast_fusion.3
  97.4 50.2 %all-reduce.6.cloned.1.call-done = f32[512,128]{1,0:T(8,128)} async-done(((f32[512,128]{1,0:T(8,128)}), f32[512,128]{1,0:T(8,128)}) %all-reduce.6.cloned.1.call-update) | async-done | bytes 262160 | tf_op jit(solution)/shard_map/psum | solution.py:51
  147.6 2.6 %multiply_reduce_fusion.1 = (f32[]{:T(128)}, f32[128,512]{1,0:T(8,128)S(1)}) fusion(f32[512,512]{1,0:T(8,128)S(1)} %copy-done.1, f32[512,128]{1,0:T(8,128)} %all-reduce.6.cloned.1.call-done, f32[512,128]{1,0:T(8,128)S(1)} %all_gather.7), kind=kOutput, calls=%fused_computation.26 | convolution fusion | flops 402849792 | bytes 1835012 | tf_op jit(solution)/shard_map/dot_general | solution.py:52
  150.2 12.3 %psum.45 = f32[]{:T(128)} all-reduce(f32[]{:T(128)} %get-tuple-element.8), channel_id=1, replica_groups=mesh['vox'=8,'load'=4] {'load'}, use_global_device_ids=true, to_apply=%region_5.0 | all-reduce | flops 1 | bytes 8 | tf_op jit(solution)/shard_map/psum | solution.py:53
  163.3 0.9 copy-done.3
  164.2 0.2 copy-done.5
  164.4 2.9 %add_add_fusion = (f32[1024,128]{1,0:T(8,128)}, f32[1024,128]{1,0:T(8,128)S(1)}) fusion(f32[1024,128]{1,0:T(8,128)S(1)} %copy-done.3, f32[1024]{0:T(1024)S(1)} %add.39, f32[1024]{0:T(1024)S(1)} %copy-done.14, s32[1024,128]{1,0:T(8,128)} %param.17, f32[1024,128]{1,0:T(8,128)} %copy-done.15, f32[1024,128]{1,0:T(8,128)S(1)} %copy-done.5, ...), kind=kOutput, calls=%fused_computation.35 | convolution fusion | flops 137297920 | bytes 4473344 | tf_op jit(solution)/shard_map/dot_general | solution.py:37
  167.3 1.7 convolution_bitcast_fusion.2
  169.0 50.3 %all-reduce.8.cloned.1.call-done = f32[512,128]{1,0:T(8,128)} async-done(((f32[512,128]{1,0:T(8,128)}), f32[512,128]{1,0:T(8,128)}) %all-reduce.8.cloned.1.call-update) | async-done | bytes 262160 | tf_op jit(solution)/shard_map/psum | solution.py:51
  219.3 2.6 %multiply_reduce_fusion = (f32[]{:T(128)}, f32[128,512]{1,0:T(8,128)S(1)}) fusion(f32[512,512]{1,0:T(8,128)S(1)} %copy-done.1, f32[512,128]{1,0:T(8,128)} %all-reduce.8.cloned.1.call-done, f32[512,128]{1,0:T(8,128)S(1)} %all_gather.7), kind=kOutput, calls=%fused_computation.23 | convolution fusion | flops 402849792 | bytes 1835012 | tf_op jit(solution)/shard_map/dot_general | solution.py:52
  221.9 12.3 %psum.47 = f32[]{:T(128)} all-reduce(f32[]{:T(128)} %get-tuple-element.10), channel_id=1, replica_groups=mesh['vox'=8,'load'=4] {'load'}, use_global_device_ids=true, to_apply=%region_8.0 | all-reduce | flops 1 | bytes 8 | tf_op jit(solution)/shard_map/psum | solution.py:53
  235.0 0.7 copy.20
  (37 shorter events, 0.4 us)
Async XLA Ops:
  7.2 11.2 %copy-start = (bf16[1024,512]{1,0:T(8,128)(2,1)S(1)}, bf16[1024,512]{1,0:T(8,128)(2,1)}, u32[]{:S(2)}) copy-start(bf16[1024,512]{1,0:T(8,128)(2,1)} %param.11) | copy-start | bytes 3145732
  7.2 11.2 %copy-start.7 = (f32[1024]{0:T(1024)S(1)}, f32[1024]{0:T(1024)}, u32[]{:S(2)}) copy-start(f32[1024]{0:T(1024)} %param.12) | copy-start | bytes 12292
  7.2 11.2 %copy-start.9 = (f32[1024]{0:T(1024)S(1)}, f32[1024]{0:T(1024)}, u32[]{:S(2)}) copy-start(f32[1024]{0:T(1024)} %param.13) | copy-start | bytes 12292
  7.2 70.0 %all-reduce.4.cloned.1.call-start = ((), (), s32[]{:S(2)}) async-start(), calls=%async_computation | async-start | bytes 524288 | tf_op jit(solution)/shard_map/psum | solution.py:51
  18.4 0.7 copy-start.8
  18.4 0.7 copy-start.10
  19.1 2.3 copy-start.11
  19.1 2.3 copy-start.14
  20.6 0.8 copy-start.4
  21.4 1.9 copy-start.6
  23.1 54.0 %copy-start.1 = (f32[512,512]{1,0:T(8,128)S(1)}, f32[512,512]{1,0:T(8,128)}, u32[]{:S(2)}) copy-start(f32[512,512]{1,0:T(8,128)} %param.21) | copy-start | bytes 3145732
  23.1 124.5 %all-reduce.6.cloned.1.call-start = ((), (), s32[]{:S(2)}) async-start(), calls=%async_computation.1 | async-start | bytes 524288 | tf_op jit(solution)/shard_map/psum | solution.py:51
  32.7 60.0 %copy-start.2 = (f32[1024,128]{1,0:T(8,128)S(1)}, f32[1024,128]{1,0:T(8,128)}, u32[]{:S(2)}) copy-start(f32[1024,128]{1,0:T(8,128)} %param.18) | copy-start | bytes 1572868
  92.7 2.9 %copy-start.12 = (s32[1024,128]{1,0:T(8,128)S(1)}, s32[1024,128]{1,0:T(8,128)}, u32[]{:S(2)}) copy-start(s32[1024,128]{1,0:T(8,128)} %param.17) | copy-start | bytes 1572868
  94.8 0.8 copy-start.15
  97.3 122.0 %all-reduce.8.cloned.1.call-start = ((), (), s32[]{:S(2)}) async-start(), calls=%async_computation.2 | async-start | bytes 524288 | tf_op jit(solution)/shard_map/psum | solution.py:51
  163.2 1.0 copy-start.3
  163.2 1.2 copy-start.5
  164.4 2.9 %copy-start.13 = (s32[1024,128]{1,0:T(8,128)S(1)}, s32[1024,128]{1,0:T(8,128)}, u32[]{:S(2)}) copy-start(s32[1024,128]{1,0:T(8,128)} %param.17) | copy-start | bytes 1572868
Sparse Core Ops, SparseCore 0:
  23.3 53.8 all-reduce.3
  97.4 50.1 all-reduce.5
  169.1 50.1 all-reduce.7
where the time goes:
time: 243 us; the launch traced here: 242 us
  waiting for transfers between devices  145 us (60%)
  blocking collectives  57.4 us (24%)
  matrix products  19.4 us (8%)
  between operations  15.9 us (7%)
  local copies, waits for them, and re-layouts  4.23 us (2%)
    psum x3, waiting for transfers between devices, shards(): resid = lax.psum(partial_sum, 'vox') - force_all  145 us
    psum x3, blocking collectives, shards(): spread = lax.psum(jnp.sum(delta * delta), 'load') / (M * load_point_total)  36.9 us
    all_gather x1, blocking collectives, shards(): lax.all_gather(starting_weights, 'vox', axis=0, tiled=True)  11.1 us
    all_gather x1, blocking collectives, shards(): lax.all_gather(applied_reduced_vector, 'vox', axis=0, tiled=True)  9.4 us
    dot_general x3, matrix products, shards(): jnp.dot(approx_tangent_inverse, resid, precision=lax.Precision.HIGHEST)  7.79 us
    dot_general x3, matrix products, shards(): jnp.dot(reduced_shape_matrix, xi_now.astype(jnp.bfloat16), preferred_elem...  6.48 us
    dot_general x3, matrix products, shards(): lax.dot_general(reduced_shape_matrix, stress, (((0,), (0,)), ((), ())), p...  5.13 us
  transfers between devices with their start and end apart: 3, of which 3 were waited for; matrix products, arithmetic and copies ran while one was open for 0% of the time, Pallas kernels for 0%

commit v1 on v0

--- a/solution.py
+++ b/solution.py
@@ -1,13 +1,260 @@
+import functools
+
 import jax
 import jax.numpy as jnp
 from jax import lax
+from jax.experimental import pallas as pl
+from jax.experimental.pallas import tpu as pltpu
 from jax.sharding import PartitionSpec as P
 
-M = 512
 ITERS = 3
-
-
-def shards(
+LANES = 128
+MESH = pl.DeviceIdType.MESH
+F32, BF16 = jnp.float32, jnp.bfloat16
+NN = (((1,), (0,)), ((), ()))
+
+
+def dot(a, b):
+    return lax.dot_general(a, b, NN, preferred_element_type=F32)
+
+
+def newton(
+    n, nl, iters,
+    a_hbm, young_ref, work_ref, flow_ref, dil_ref, heat_ref, flags_hbm, start_hbm, xi_ref, applied_ref, t_hbm,
+    xi_out, plastic_out,
+    a_s, t_s, flags_s, q_s, e_s, y_s, yinv_s, c_s, heat_s, t_hi, t_lo,
+    xi_g, app_s, app_t, xi_t, xib, s_t, part, precv, dbuf, dlast_src, dlast, turn, zbuf, cbuf,
+    load_sem, xi_send, xi_recv, p_send, p_recv, d_send, d_recv, z_send, z_recv, c_send, c_recv,
+):
+    me, my_load = lax.axis_index("vox"), lax.axis_index("load")
+    rows, modes = a_s.shape
+    own, points = xi_ref.shape
+    per = points // n
+
+    def to(k):
+        return lax.rem(me + k, n)
+
+    def fro(k):
+        return lax.rem(me + n - k, n)
+
+    def z_to(k):
+        return lax.rem(my_load + k, nl)
+
+    def z_fro(k):
+        return lax.rem(my_load + nl - k, nl)
+
+    def lane_of(j):
+        return pl.multiple_of(j * own // LANES * LANES, LANES)
+
+    def send(src, dst, send_sem, recv_sem, axis, target):
+        return pltpu.make_async_remote_copy(
+            src_ref=src, dst_ref=dst, send_sem=send_sem, recv_sem=recv_sem,
+            device_id={axis: target}, device_id_type=MESH,
+        )
+
+    barrier = pltpu.get_barrier_semaphore()
+    for k in range(1, n):
+        pl.semaphore_signal(barrier, inc=1, device_id={"vox": to(k)}, device_id_type=MESH)
+    for k in range(1, nl):
+        pl.semaphore_signal(barrier, inc=1, device_id={"load": z_to(k)}, device_id_type=MESH)
+    loads = [
+        pltpu.make_async_copy(s, d, load_sem.at[i])
+        for i, (s, d) in enumerate(((flags_hbm, flags_s), (start_hbm, q_s), (t_hbm, t_s), (a_hbm, a_s)))
+    ]
+    for c in loads:
+        c.start()
+    pl.semaphore_wait(barrier, n + nl - 2)
+
+    xi_sends = [
+        send(xi_ref, xi_g.at[me], xi_send.at[k - 1], xi_recv.at[k - 1], "vox", to(k)) for k in range(1, n)
+    ]
+    for c in xi_sends:
+        c.start()
+    xi_g[me] = xi_ref[...]
+
+    for c in loads[:2]:
+        c.wait()
+    count = rows // LANES
+    stack = [young_ref[...], work_ref[...], flow_ref[...], dil_ref[...]]
+    packed = jnp.concatenate(stack + [jnp.zeros((LANES - 4 * count, LANES), F32)], axis=0).T
+    for i in range(count):
+        at = pl.ds(i * LANES, LANES)
+        young, work, flow, dil = (
+            jnp.broadcast_to(packed[:, p * count + i : p * count + i + 1], (LANES, points)) for p in range(4)
+        )
+        warm = dil * heat_ref[...]
+        e_s[at, :] = young
+        y_s[at, :] = flow
+        yinv_s[at, :] = 1.0 / flow
+        c_s[at, :] = flags_s[at, :].astype(F32) / (young + work)
+        heat_s[at, :] = warm
+        q_s[at, :] = q_s[at, :] + warm
+    app_s[...] = jnp.zeros_like(app_s)
+    app_s[me] = applied_ref[...]
+    app_t[...] = app_s[...].reshape(modes, points).T
+    loads[2].wait()
+    for i in range(modes // LANES):
+        at = pl.ds(i * LANES, LANES)
+        block = t_s[at, :].T
+        high = block.astype(BF16)
+        t_hi[:, at] = high
+        t_lo[:, at] = (block - high.astype(F32)).astype(BF16)
+    loads[3].wait()
+
+    for k in range(1, n):
+        send(xi_ref, xi_g.at[fro(k)], xi_send.at[k - 1], xi_recv.at[k - 1], "vox", to(k)).wait_recv()
+    xib[...] = xi_g[...].reshape(modes, points).astype(BF16)
+
+    chunk = 256
+    for it in range(iters):
+        final = it == iters - 1
+        for i in range(rows // chunk):
+            at = pl.ds(i * chunk, chunk)
+            e, q = e_s[at, :], q_s[at, :]
+            trial = e * (dot(a_s[at, :], xib[...]) - q)
+            excess = trial - y_s[at, :] * jnp.tanh(trial * yinv_s[at, :])
+            increment = c_s[at, :] * excess
+            q = q + increment
+            if final:
+                plastic_out[at, :] = q - heat_s[at, :]
+            else:
+                q_s[at, :] = q
+            s_t[:, at] = (trial - e * increment).astype(BF16).T
+        if it > 0:
+            for c in p_copies:
+                c.wait_send()
+        part[...] = (dot(s_t[...], a_s[...]) - app_t[...]).reshape(n, per, modes)
+
+        p_copies = [
+            send(part.at[to(k)], precv.at[it, k - 1], p_send.at[it, k - 1], p_recv.at[it, k - 1], "vox", to(k))
+            for k in range(1, n)
+        ]
+        for c in p_copies:
+            c.start()
+        if it == 0:
+            for c in xi_sends:
+                c.wait_send()
+            xi_t[...] = xi_g[...].reshape(modes, points).T
+        resid = part[me]
+        for k in range(1, n):
+            p_copies[k - 1].wait_recv()
+            resid = resid + precv[it, k - 1]
+        r_hi = resid.astype(BF16)
+        r_lo = (resid - r_hi.astype(F32)).astype(BF16)
+        both = dot(jnp.concatenate([r_hi, r_lo], axis=0), t_hi[...])
+        delta = both[:per] + (both[per:] + dot(r_hi, t_lo[...]))
+
+        square = delta * delta
+        tile = jnp.sum(square.reshape(per // 8, 8, modes), axis=0)
+        zbuf[it, my_load] = sum(tile[:, j * LANES : (j + 1) * LANES] for j in range(modes // LANES))
+        z_copies = [
+            send(zbuf.at[it, my_load], zbuf.at[it, my_load], z_send.at[it, k - 1], z_recv.at[it, k - 1], "load", z_to(k))
+            for k in range(1, nl)
+        ]
+        for c in z_copies:
+            c.start()
+        if final:
+            dlast_src[...] = delta
+            dlast[me] = dlast_src[:, pl.ds(lane_of(me), LANES)]
+            d_copies = [
+                send(
+                    dlast_src.at[:, pl.ds(lane_of(to(k)), LANES)], dlast.at[me],
+                    d_send.at[it, k - 1], d_recv.at[it, k - 1], "vox", to(k),
+                )
+                for k in range(1, n)
+            ]
+        else:
+            dbuf[it, me] = delta
+            d_copies = [
+                send(dbuf.at[it, me], dbuf.at[it, me], d_send.at[it, k - 1], d_recv.at[it, k - 1], "vox", to(k))
+                for k in range(1, n)
+            ]
+        for c in d_copies:
+            c.start()
+        for k in range(1, nl):
+            send(
+                zbuf.at[it, my_load], zbuf.at[it, z_fro(k)], z_send.at[it, k - 1], z_recv.at[it, k - 1], "load", z_to(k)
+            ).wait_recv()
+        cbuf[it, me] = jnp.sum(zbuf[it], axis=0)
+        c_copies = [
+            send(cbuf.at[it, me], cbuf.at[it, me], c_send.at[it, k - 1], c_recv.at[it, k - 1], "vox", to(k))
+            for k in range(1, n)
+        ]
+        for c in c_copies:
+            c.start()
+        for k in range(1, n):
+            if final:
+                here = send(
+                    dlast_src.at[:, pl.ds(lane_of(to(k)), LANES)], dlast.at[fro(k)],
+                    d_send.at[it, k - 1], d_recv.at[it, k - 1], "vox", to(k),
+                )
+            else:
+                here = send(
+                    dbuf.at[it, me], dbuf.at[it, fro(k)], d_send.at[it, k - 1], d_recv.at[it, k - 1], "vox", to(k)
+                )
+            here.wait_recv()
+        for k in range(1, n):
+            send(
+                cbuf.at[it, me], cbuf.at[it, fro(k)], c_send.at[it, k - 1], c_recv.at[it, k - 1], "vox", to(k)
+            ).wait_recv()
+        spread = jnp.sum(jnp.sum(cbuf[it], axis=0), keepdims=True) / (modes * points * nl)
+        damp = 1.0 / (1.0 + spread)
+        if final:
+            last = xi_t[:, pl.ds(lane_of(me), LANES)] - dlast[...].reshape(points, LANES) * damp
+            turn[...] = last.T
+            xi_out[...] = turn[pl.ds(pl.multiple_of(lax.rem(me * own, LANES), own), own), :]
+        else:
+            now = xi_t[...] - dbuf[it].reshape(points, modes) * damp
+            xi_t[...] = now
+            xib[...] = now.T.astype(BF16)
+        for c in z_copies + d_copies + c_copies:
+            c.wait_send()
+    for c in p_copies:
+        c.wait_send()
+
+
+def fused(n, nl, a, young, work, flow, dil, heat, flags, start, xi, applied, tangent):
+    rows, modes = a.shape
+    own, points = xi.shape
+    per, count = points // n, rows // LANES
+    as_rows = [v.reshape(count, LANES) for v in (young, work, flow, dil)]
+    full = lambda dtype: pltpu.VMEM((rows, points), dtype)
+    dma = lambda *shape: pltpu.SemaphoreType.DMA(shape)
+    in_vmem, in_hbm = pl.BlockSpec(memory_space=pltpu.VMEM), pl.BlockSpec(memory_space=pl.ANY)
+    return pl.pallas_call(
+        functools.partial(newton, n, nl, ITERS),
+        out_shape=(jax.ShapeDtypeStruct((own, points), F32), jax.ShapeDtypeStruct((rows, points), F32)),
+        in_specs=[in_hbm] + [in_vmem] * 5 + [in_hbm] * 2 + [in_vmem] * 2 + [in_hbm],
+        out_specs=(in_vmem, in_vmem),
+        scratch_shapes=[
+            pltpu.VMEM((rows, modes), BF16), pltpu.VMEM((modes, modes), F32), full(jnp.int32),
+            full(F32), full(F32), full(F32), full(F32), full(F32), full(F32),
+            pltpu.VMEM((modes, modes), BF16), pltpu.VMEM((modes, modes), BF16),
+            pltpu.VMEM((n, own, points), F32), pltpu.VMEM((n, own, points), F32),
+            pltpu.VMEM((points, modes), F32), pltpu.VMEM((points, modes), F32),
+            pltpu.VMEM((modes, points), BF16), pltpu.VMEM((points, rows), BF16),
+            pltpu.VMEM((n, per, modes), F32), pltpu.VMEM((ITERS, n - 1, per, modes), F32),
+            pltpu.VMEM((ITERS - 1, n, per, modes), F32), pltpu.VMEM((per, modes), F32),
+            pltpu.VMEM((n, per, LANES), F32), pltpu.VMEM((LANES, points), F32),
+            pltpu.VMEM((ITERS, nl, 8, LANES), F32), pltpu.VMEM((ITERS, n, 8, LANES), F32),
+            dma(4), dma(n - 1), dma(n - 1), dma(ITERS, n - 1), dma(ITERS, n - 1), dma(ITERS, n - 1),
+            dma(ITERS, n - 1), dma(ITERS, nl - 1), dma(ITERS, nl - 1), dma(ITERS, n - 1), dma(ITERS, n - 1),
+        ],
+        compiler_params=pltpu.CompilerParams(
+            collective_id=0, has_side_effects=True, vmem_limit_bytes=40 * 1024 * 1024
+        ),
+    )(a, *as_rows, heat.reshape(1, points), flags, start, xi, applied, tangent)
+
+
+def fits(n, nl, a, xi):
+    (rows, modes), (own, points) = a.shape, xi.shape
+    return (
+        n > 1 and nl > 1 and rows % 256 == 0 and 4 * rows <= LANES * LANES and modes % LANES == 0
+        and points == LANES and points % (8 * n) == 0 and own % 8 == 0 and LANES % own == 0
+    )
+
+
+def plain(
     reduced_shape_matrix,
     young_modulus,
     work_stiffening_modulus,
@@ -50,10 +297,17 @@
         )
         resid = lax.psum(partial_sum, "vox") - force_all
         delta = jnp.dot(approx_tangent_inverse, resid, precision=lax.Precision.HIGHEST)
-        spread = lax.psum(jnp.sum(delta * delta), "load") / (M * load_point_total)
+        spread = lax.psum(jnp.sum(delta * delta), "load") / (starting_weights.shape[0] * lax.axis_size("vox") * load_point_total)
         xi_now = xi_now - delta / (1.0 + spread)
     mine = lax.dynamic_slice_in_dim(xi_now, lax.axis_index("vox") * own_rows, own_rows, 0)
     return (mine, plastic)
+
+
+def shards(*args):
+    n, nl = lax.axis_size("vox"), lax.axis_size("load")
+    if fits(n, nl, args[0], args[8]):
+        return fused(n, nl, *args)
+    return plain(*args)
 
 
 def solution(mesh):

time: 243 us -> 60.2 us (0.25)
  waiting for transfers between devices: 145 us -> 0 us
  blocking collectives: 57.4 us -> 0 us
  Pallas kernels: 0 us -> 49.5 us
  matrix products: 19.4 us -> 0 us
  between operations: 15.9 us -> 0.68 us
  local copies, waits for them, and re-layouts: 4.23 us -> 9.51 us
    psum x3 -> x0, waiting for transfers between devices: 145 us -> none  [shards(): resid = lax.psum(partial_sum, 'vox') - force_all]
    pallas_call x0 -> x1, Pallas kernels: none -> 49.5 us  [fused(): pl.pallas_call(functools.partial(newton, n, nl, ITERS), out_shape=(jax.Sh...]
    psum x3 -> x0, blocking collectives: 36.9 us -> none  [shards(): spread = lax.psum(jnp.sum(delta * delta), 'load') / (M * load_point_total)]
    all_gather x2 -> x0, blocking collectives: 20.5 us -> none  [the longest x1 11.1 us: shards(): lax.all_gather(starting_weights, 'vox', axis=0, tiled=True)]
    dot_general x9 -> x0, matrix products: 19.4 us -> none  [the longest x3 7.79 us: shards(): jnp.dot(approx_tangent_inverse, resid, precision=lax.Precision.HIGHEST)]
    unnamed x33 -> x24, local copies, waits for them, and re-layouts: 4.1 us -> 9.51 us
  transfers between devices with their start and end apart: 3 -> 0, of which waited for: 3 -> 0; matrix products, arithmetic and copies ran while one was open for 0% -> 0% of each run, Pallas kernels for 0% -> 0%
where the time goes in v1:
time: 60.2 us; the launch traced here: 59.7 us
  Pallas kernels  49.5 us (82%)
  local copies, waits for them, and re-layouts  9.51 us (16%)
  between operations  0.68 us (1%)
    pallas_call x1, Pallas kernels, fused(): pl.pallas_call(functools.partial(newton, n, nl, ITERS), out_shape=(jax.Sh...  49.5 us
    unnamed x24, local copies, waits for them, and re-layouts  9.51 us

profile of v1, /device:TPU:0, one launch (start us, length us, event | category | flops | bytes accessed | tf_op | source)
XLA Modules:
  0.0 59.7 jit_solution(5527215388387377802)
XLA Ops:
  0.6 0.0 copy-start.7
  0.6 0.0 copy-start.6
  0.7 0.0 copy-start.10
  0.7 0.7 %copy-done.7 = f32[1024]{0:T(1024)S(1)} copy-done((f32[1024]{0:T(1024)S(1)}, f32[1024]{0:T(1024)}, u32[]{:S(2)}) %copy-start.7) | copy-done | bytes 4120
  1.3 0.0 copy-done.6
  1.3 0.0 copy-done.10
  1.3 0.0 copy-start
  1.3 1.2 %copy-done = bf16[1024,512]{1,0:T(8,128)(2,1)S(1)} copy-done((bf16[1024,512]{1,0:T(8,128)(2,1)S(1)}, bf16[1024,512]{1,0:T(8,128)(2,1)}, u32[]{:S(2)}) %copy-start) | copy-done | bytes 1048600
  2.6 0.0 copy-start.1
  2.6 1.2 %copy-done.1 = f32[512,512]{1,0:T(8,128)S(1)} copy-done((f32[512,512]{1,0:T(8,128)S(1)}, f32[512,512]{1,0:T(8,128)}, u32[]{:S(2)}) %copy-start.1) | copy-done | bytes 1048600
  3.8 0.0 copy-start.2
  3.8 1.0 %copy-done.2 = s32[1024,128]{1,0:T(8,128)S(1)} copy-done((s32[1024,128]{1,0:T(8,128)S(1)}, s32[1024,128]{1,0:T(8,128)}, u32[]{:S(2)}) %copy-start.2) | copy-done | bytes 524312
  4.8 0.0 copy-start.3
  4.8 1.0 %copy-done.3 = f32[1024,128]{1,0:T(8,128)S(1)} copy-done((f32[1024,128]{1,0:T(8,128)S(1)}, f32[1024,128]{1,0:T(8,128)}, u32[]{:S(2)}) %copy-start.3) | copy-done | bytes 524312
  5.9 0.0 copy-start.4
  5.9 0.8 %copy-done.4 = f32[64,128]{1,0:T(8,128)S(1)} copy-done((f32[64,128]{1,0:T(8,128)S(1)}, f32[64,128]{1,0:T(8,128)}, u32[]{:S(2)}) %copy-start.4) | copy-done | bytes 32792
  6.6 0.0 copy-start.5
  6.6 0.8 %copy-done.5 = f32[64,128]{1,0:T(8,128)S(1)} copy-done((f32[64,128]{1,0:T(8,128)S(1)}, f32[64,128]{1,0:T(8,128)}, u32[]{:S(2)}) %copy-start.5) | copy-done | bytes 32792
  7.4 0.0 copy-start.8
  7.4 0.7 %copy-done.8 = f32[1024]{0:T(1024)S(1)} copy-done((f32[1024]{0:T(1024)S(1)}, f32[1024]{0:T(1024)}, u32[]{:S(2)}) %copy-start.8) | copy-done | bytes 4120
  8.1 0.7 %copy-done.9 = f32[1024]{0:T(1024)S(1)} copy-done((f32[1024]{0:T(1024)S(1)}, f32[1024]{0:T(1024)}, u32[]{:S(2)}) %copy-start.9) | copy-done | bytes 4120
  8.8 49.5 %shard_map.122 = (f32[64,128]{1,0:T(8,128)S(1)}, f32[1024,128]{1,0:T(8,128)S(1)}) custom-call(bf16[1024,512]{1,0:T(8,128)(2,1)S(1)} %copy-done, f32[8,128]{1,0:T(8,128)S(1)} %bitcast.5, f32[8,128]{1,0:T(8,128)S(1)} %bitcast.6, f32[8,128]{1,0:T(8,128)S(1)} %bitcast.7, f32[8,128]{1,0:T(8,128)S(1)} %bitcast.8, f32[1,128]{1,0:T(1,128)S(1)} %bitcast.9, ...), custom_call_target="tpu_custom_call" | custom-call | tf_op jit(solution)/shard_map/pallas_call | solution.py:224
  58.3 0.6 %copy.15 = f32[64,128]{1,0:T(8,128)} copy(f32[64,128]{1,0:T(8,128)S(1)} %get-tuple-element.4) | data formatting | bytes 65536
  58.9 0.8 %copy.16 = f32[1024,128]{1,0:T(8,128)} copy(f32[1024,128]{1,0:T(8,128)S(1)} %get-tuple-element.5) | data formatting | bytes 1048576
  (1 shorter events, 0.0 us)
Async XLA Ops:
  0.6 0.7 %copy-start.7 = (f32[1024]{0:T(1024)S(1)}, f32[1024]{0:T(1024)}, u32[]{:S(2)}) copy-start(f32[1024]{0:T(1024)} %param.13) | copy-start | bytes 12292
  0.6 0.7 %copy-start.6 = (f32[1024]{0:T(1024)S(1)}, f32[1024]{0:T(1024)}, u32[]{:S(2)}) copy-start(f32[1024]{0:T(1024)} %param.12) | copy-start | bytes 12292
  0.7 0.7 %copy-start.10 = (f32[128]{0:T(128)S(1)}, f32[128]{0:T(128)}, u32[]{:S(2)}) copy-start(f32[128]{0:T(128)} %param.16) | copy-start | bytes 1540
  1.3 1.2 %copy-start = (bf16[1024,512]{1,0:T(8,128)(2,1)S(1)}, bf16[1024,512]{1,0:T(8,128)(2,1)}, u32[]{:S(2)}) copy-start(bf16[1024,512]{1,0:T(8,128)(2,1)} %a_hbm.1) | copy-start | bytes 3145732
  2.6 1.2 %copy-start.1 = (f32[512,512]{1,0:T(8,128)S(1)}, f32[512,512]{1,0:T(8,128)}, u32[]{:S(2)}) copy-start(f32[512,512]{1,0:T(8,128)} %t_hbm.1) | copy-start | bytes 3145732
  3.8 1.0 %copy-start.2 = (s32[1024,128]{1,0:T(8,128)S(1)}, s32[1024,128]{1,0:T(8,128)}, u32[]{:S(2)}) copy-start(s32[1024,128]{1,0:T(8,128)} %flags_hbm.1) | copy-start | bytes 1572868
  4.8 1.0 %copy-start.3 = (f32[1024,128]{1,0:T(8,128)S(1)}, f32[1024,128]{1,0:T(8,128)}, u32[]{:S(2)}) copy-start(f32[1024,128]{1,0:T(8,128)} %start_hbm.1) | copy-start | bytes 1572868
  5.9 0.8 %copy-start.4 = (f32[64,128]{1,0:T(8,128)S(1)}, f32[64,128]{1,0:T(8,128)}, u32[]{:S(2)}) copy-start(f32[64,128]{1,0:T(8,128)} %xi_ref.1) | copy-start | bytes 98308
  6.6 0.8 %copy-start.5 = (f32[64,128]{1,0:T(8,128)S(1)}, f32[64,128]{1,0:T(8,128)}, u32[]{:S(2)}) copy-start(f32[64,128]{1,0:T(8,128)} %applied_ref.1) | copy-start | bytes 98308
  7.4 0.7 %copy-start.8 = (f32[1024]{0:T(1024)S(1)}, f32[1024]{0:T(1024)}, u32[]{:S(2)}) copy-start(f32[1024]{0:T(1024)} %param.14) | copy-start | bytes 12292
  8.1 0.7 %copy-start.9 = (f32[1024]{0:T(1024)S(1)}, f32[1024]{0:T(1024)}, u32[]{:S(2)}) copy-start(f32[1024]{0:T(1024)} %param.15) | copy-start | bytes 12292
